TPU v7x, 128 devices: a whole 4x4x4 slice. The times are simulated.
128 devices in a mesh: gx: 16 (over y, x), gz: 8 (over z, core).
Axes of the slice: x: 4, y: 4, z: 4, core: 2. Of those that a mesh axis runs over, the one named last changes fastest.
Arguments:
- populations: float32 [19, 128, 256, 128], P(None, 'gx', 'gz'), may hold values from 0 to 1, as said below
- thermal: float32 [7, 128, 256, 128], P(None, 'gx', 'gz'), may hold values from 0 to 1, as said below
- solid_blocks: float32 [16384, 128], P(('gx', 'gz')), may hold values from 0.05 to 0.95
- centre_dev: int32 [3, 16384, 1], P(None, ('gx', 'gz')), may hold values from 0 to 127; in each aligned block of 128 rows (0 to 127, 128 to 255, ..., all dimensions but the last counted through in order) at most 2 rows name the same one
- centre_col: int32 [3, 16384], P(None, ('gx', 'gz')), may hold values from 0 to 255
- grain_velocity: int32 [3, 3, 16384], P(None, None, ('gx', 'gz')), may hold values from -3200 to 3200
- capture: int32 [3, 16384], P(None, ('gx', 'gz')), may hold values 0 or 1
Outputs:
- flow_out: float32 [19, 128, 256, 128], P(None, 'gx', 'gz')
- heat_out: float32 [7, 128, 256, 128], P(None, 'gx', 'gz')
- solid_out: float32 [16384, 128], P(('gx', 'gz'))
- grain_drag: float32 [3, 16384], P(None, ('gx', 'gz'))
Inputs may be any that keep to these rules, and one draw needn't show every extreme that they name: `centre_dev`: in every step the 128 grains held by one device name each device at most 2 times, and some device exactly 2 times. `populations`: every population is positive. `thermal`: every population is positive.
All inputs are finite; a program needn't handle non-finite values. No bound on the sum of `capture` on one device may be relied on, other than what follows from the above.
Results may differ from a plain program's by a relative error of at most 0.0003.
Values sent between devices are 32-bit elements; how exact they have to be, the bound alone decides.
A program may use at most 128 MiB of HBM per device.

v0:
```python
import functools

import jax
import jax.numpy as jnp
from jax import lax
from jax.experimental import pallas as pl
from jax.experimental.pallas import tpu as pltpu
from jax.sharding import PartitionSpec as P

FLOW = [
    (0, 0, 0), (1, 0, 0), (-1, 0, 0), (0, 1, 0), (0, -1, 0), (0, 0, 1), (0, 0, -1),
    (1, 1, 0), (-1, -1, 0), (1, -1, 0), (-1, 1, 0), (1, 0, 1), (-1, 0, -1), (1, 0, -1),
    (-1, 0, 1), (0, 1, 1), (0, -1, -1), (0, 1, -1), (0, -1, 1),
]
HEAT = [(0, 0, 0), (1, 0, 0), (-1, 0, 0), (0, 1, 0), (0, -1, 0), (0, 0, 1), (0, 0, -1)]
ORDER = [1, 7, 9, 20, 11, 13, 2, 8, 10, 21, 12, 14, 5, 15, 18, 24, 6, 16, 17, 25, 0, 3, 4, 19, 22, 23]
PLACE = [ORDER.index(k) for k in range(26)]
PAIRS = [(1, 2), (3, 4), (5, 6), (7, 8), (9, 10), (11, 12), (13, 14), (15, 16), (17, 18)]
TAU = 0.8
TAU_T = 0.7
BETA = 0.5
BUOY = 0.01
LATENT = 0.5
DRAG_SCALE = 40.0
VEL_UNIT = 1.0 / 32768.0
F32 = jnp.float32
BF16 = jnp.bfloat16
MESH = pl.DeviceIdType.MESH
TOP = 8


def dotted(velocity, vector):
    total = None
    for axis_id in range(3):
        if velocity[axis_id] == 1:
            total = vector[axis_id] if total is None else total + vector[axis_id]
        elif velocity[axis_id] == -1:
            total = -vector[axis_id] if total is None else total - vector[axis_id]
    return total


def halves(block):
    high = block.astype(BF16)
    return high, (block - high.astype(F32)).astype(BF16)


def product(left, right):
    return jnp.dot(left, right, preferred_element_type=F32)


def lanes_of(shape):
    return lax.broadcasted_iota(jnp.int32, shape, 1).astype(F32)


def rows_of(shape):
    return lax.broadcasted_iota(jnp.int32, shape, 0).astype(F32)


def chosen(condition):
    return jnp.where(condition, 1.0, 0.0).astype(F32)


def kernel(
    sizes,
    pop, th, solid_in, cdev, ccol, gvel, cap,
    flow_out, heat_out, solid_out, drag_out,
    w0, w1, w2, w3, dens, speeds, temps, mx_b, speed_b, cover,
    table, pick, pick_t, disp, disp_t, caps, spread, solid, drags, gathered,
    out0_s, out0_r, out1_s, out1_r, out2_s, out2_r,
    back0_s, back0_r, back1_s, back1_r, back2_s, back2_r,
    in_sem, out_sem, halo_ss, halo_rs, grain_ss, grain_rs,
):
    n_gx, n_gz = sizes
    n_dev = n_gx * n_gz
    gx, gz = lax.axis_index("gx"), lax.axis_index("gz")
    me = gx * n_gz + gz
    states = (w0, w1, w2, w3)
    width_x, width_z = dens.shape[0], dens.shape[1]
    grains = solid.shape[0]

    def peers(body):
        def group(i, carry):
            k = 1 + lax.rem(n_gx // 2 + 1 + i, n_gx - 1)
            there = lax.rem(gx + k, n_gx)
            for d in (4, 3, 5, 2, 6, 1, 7, 0):
                body(there, lax.rem(gz + d, n_gz))
            return carry

        lax.fori_loop(0, n_gx - 1, group, 0)
        for d in (4, 3, 5, 2, 6, 1, 7):
            body(gx, lax.rem(gz + d, n_gz))

    barrier = pltpu.get_barrier_semaphore()
    peers(lambda x, z: pl.semaphore_signal(barrier, inc=1, device_id=(x, z), device_id_type=MESH))

    loads = []
    for k in range(26):
        source = pop.at[k] if k < 19 else th.at[k - 19]
        loads.append(
            pltpu.make_async_copy(
                source, w0.at[PLACE[k], pl.ds(1, width_x), pl.ds(TOP, width_z), :], in_sem.at[k]
            )
        )
        loads[-1].start()

    def send_rows(which, source, target):
        def one(x, z):
            pltpu.make_async_remote_copy(
                src_ref=source.at[x * n_gz + z],
                dst_ref=target.at[me],
                send_sem=grain_ss.at[which],
                recv_sem=grain_rs.at[which],
                device_id=(x, z),
                device_id_type=MESH,
            ).start()

        peers(one)
        target[pl.ds(me, 1)] = source[pl.ds(me, 1)]

    def rows_sent(which, source):
        part = source.at[pl.ds(0, n_dev - 1)]
        pltpu.make_async_copy(part, part, grain_ss.at[which]).wait()

    def rows_here(which, target):
        part = target.at[pl.ds(0, n_dev - 1)]
        pltpu.make_async_copy(part, part, grain_rs.at[which]).wait()

    square = (grains, grains)
    lane, row = lanes_of(square), rows_of(square)
    table[...] = jnp.zeros(table.shape, F32)
    for t in range(3):
        table[8 * t : 8 * t + 1, :] = ccol[t : t + 1, :].astype(F32)
        table[8 * t + 1 : 8 * t + 2, :] = cap[t : t + 1, :].astype(F32)
        for c in range(3):
            table[8 * t + 2 + c : 8 * t + 3 + c, :] = gvel[3 * t + c : 3 * t + c + 1, :].astype(F32)
    facts = table[...].T
    facts_moved = pltpu.roll(facts, grains // 2, axis=1)
    details = jnp.zeros((n_dev, grains), F32)
    for t in range(3):
        goal = jnp.broadcast_to(cdev[t : t + 1, :].astype(F32), square)
        goal_t = goal.T
        same = goal == goal_t
        rank = jnp.sum(chosen(same & (row < lane)), axis=0, keepdims=True)
        rank_t = jnp.sum(chosen(same & (lane < row)), axis=1, keepdims=True)
        for s in range(2):
            d = chosen((row == goal) & (rank == s)).astype(BF16)
            d_t = chosen((lane == goal_t) & (rank_t == s)).astype(BF16)
            for half in range(2):
                disp[t, s * n_dev : (s + 1) * n_dev, half * grains : (half + 1) * grains] = d
                at = (2 * half + s) * n_dev
                disp_t[t, :, at : at + n_dev] = d_t
            first = 64 * s + 8 * t
            mine = jnp.where(
                (lane >= first) & (lane < first + 8), facts_moved if s else facts, 0.0
            )
            high, low = halves(mine)
            details = details + product(d, high) + product(d, low)
        caps[t] = jnp.broadcast_to(facts[:, 8 * t + 1 : 8 * t + 2], square)

    def packed(t):
        high, low = halves(solid[...])
        return product(disp[t], jnp.concatenate([high, low], axis=0))

    solid[...] = solid_in[...]
    rows = packed(0)
    out0_s[:, 0, 0:128] = rows[0:n_dev]
    out0_s[:, 0, 128:256] = rows[n_dev : 2 * n_dev]
    out0_s[:, 0, 256:384] = details

    pl.semaphore_wait(barrier, n_dev - 1)
    send_rows(0, out0_s, out0_r)

    def moments(t, x):
        w = states[t]

        def at(k):
            return w[PLACE[k], x + 1, TOP : TOP + width_z, :]

        density = at(0)
        momentum = [None, None, None]
        for a, b in PAIRS:
            one, two = at(a), at(b)
            density = density + (one + two)
            apart = one - two
            for c in range(3):
                if FLOW[a][c] == 1:
                    momentum[c] = apart if momentum[c] is None else momentum[c] + apart
                elif FLOW[a][c] == -1:
                    momentum[c] = momentum[c] - apart
        temper = at(19)
        for k in range(20, 26):
            temper = temper + at(k)
        dens[x] = density
        temps[x] = temper
        inverse = 1.0 / density
        for c in range(3):
            speed = momentum[c] * inverse
            speeds[c, x] = speed
            high, low = halves(speed)
            speed_b[x, :, c * 128 : (c + 1) * 128] = high
            speed_b[width_x + x, :, c * 128 : (c + 1) * 128] = low
        high, low = halves(jnp.maximum(1.0 - temper, 0.0))
        mx_b[x] = high
        mx_b[width_x + x] = low

    def all_moments(t):
        def one(x, carry):
            moments(t, x)
            return carry

        lax.fori_loop(0, width_x, one, 0)

    cells = width_x * width_z

    def make_picks(t):
        detail = out0_r[:, 0, 256:384]
        detail_t = detail.T
        for s in range(2):
            at = 64 * s + 8 * t
            p = chosen(lanes_of((n_dev, cells)) == detail[:, at : at + 1]).astype(BF16)
            p_t = chosen(rows_of((cells, n_dev)) == detail_t[at : at + 1, :]).astype(BF16)
            for half in range(2):
                pick[t, s * n_dev : (s + 1) * n_dev, half * cells : (half + 1) * cells] = p
                k = (2 * half + s) * n_dev
                pick_t[t, :, k : k + n_dev] = p_t

    def gather_mx(t):
        return product(pick[t], mx_b[...].reshape(2 * cells, 128))

    def blocks_here(t, s):
        if t == 0:
            return out0_r[:, 0, s * 128 : (s + 1) * 128]
        return (out1_r if t == 1 else out2_r)[:, s, :]

    def make_cover(t):
        detail = out0_r[:, 0, 256:384]
        for s in range(2):
            block = blocks_here(t, s)
            at = 64 * s + 8 * t
            parts = [block]
            for c in range(3):
                parts.append(block * (detail[:, at + 2 + c : at + 3 + c] * VEL_UNIT))
            parts.append(detail[:, at + 1 : at + 2] * (1.0 - block))
            for c in range(5):
                high, low = halves(parts[c])
                spread[s * n_dev : (s + 1) * n_dev, c * 128 : (c + 1) * 128] = high
                spread[(2 + s) * n_dev : (3 + s) * n_dev, c * 128 : (c + 1) * 128] = low
        cover[...] = product(pick_t[t], spread[...]).reshape(width_x, width_z, 640)

    def gather_speed(t):
        gathered[...] = product(pick[t], speed_b[...].reshape(2 * cells, 384))

    def make_drag(t):
        detail = out0_r[:, 0, 256:384]
        lane_d = lanes_of((n_dev, 128))
        total = drags[...]
        for s in range(2):
            block = blocks_here(t, s)
            at = 64 * s + 8 * t
            for c in range(3):
                speed = gathered[s * n_dev : (s + 1) * n_dev, c * 128 : (c + 1) * 128]
                drag = block * (speed - detail[:, at + 2 + c : at + 3 + c] * VEL_UNIT)
                mean = jnp.sum(drag, axis=1, keepdims=True) * (BETA / 128.0)
                total = jnp.where(lane_d == 8 * (2 * t + s) + c, mean, total)
        drags[...] = total

    def collide(t, x):
        w, after = states[t], states[t + 1]
        tall = 16
        for z in range(0, width_z, tall):
            here = slice(z, z + tall)

            def put(k, value):
                velo = FLOW[k] if k < 19 else HEAT[k - 19]
                if velo[1]:
                    value = pltpu.roll(value, velo[1] % 128, axis=1)
                start = TOP + z + velo[2]
                after[PLACE[k], x + 1 + velo[0], start : start + tall, :] = value

            def at(k):
                return w[PLACE[k], x + 1, TOP + z : TOP + z + tall, :]

            density = dens[x, here, :]
            temper = temps[x, here, :]
            speed = [speeds[c, x, here, :] for c in range(3)]
            spots = [cover[x, here, c * 128 : (c + 1) * 128] for c in range(5)]
            pull = (TAU * BETA) / density
            shifted = [speed[c] + pull * (spots[1 + c] - spots[0] * speed[c]) for c in range(3)]
            shifted[2] = shifted[2] + (TAU * BUOY) * (temper - 1.0)
            square_ = shifted[0] * shifted[0] + shifted[1] * shifted[1] + shifted[2] * shifted[2]
            base18 = density * (1.0 / (18.0 * TAU)) * (1.0 - 1.5 * square_)
            base36 = 0.5 * base18
            way18 = density * (3.0 / (18.0 * TAU))
            way36 = 0.5 * way18
            keep = 1.0 - 1.0 / TAU
            put(0, 6.0 * base18 + keep * at(0))
            for a, b in PAIRS:
                along = dotted(FLOW[a], shifted)
                odd = (way18 if a < 7 else way36) * along
                even = (base18 if a < 7 else base36) + 1.5 * along * odd
                put(a, even + odd + keep * at(a))
                put(b, even - odd + keep * at(b))
            keep = 1.0 - 1.0 / TAU_T
            latent = LATENT * jnp.maximum(1.0 - temper, 0.0) * spots[4]
            warm = temper * (1.0 / TAU_T)
            even = 0.125 * (warm + latent)
            put(19, 2.0 * even + keep * at(19))
            half_warm = 0.5 * warm
            for c, axis_id in ((0, 0), (1, 1), (2, 2)):
                odd = half_warm * speed[axis_id]
                put(20 + 2 * c, even + odd + keep * at(20 + 2 * c))
                put(21 + 2 * c, even - odd + keep * at(21 + 2 * c))

    left, right = lax.rem(gx + n_gx - 1, n_gx), lax.rem(gx + 1, n_gx)
    down, up = lax.rem(gz + n_gz - 1, n_gz), lax.rem(gz + 1, n_gz)
    end_x, end_z = width_x + 1, TOP + width_z
    all_z = pl.ds(TOP, width_z)
    all_x = pl.ds(1, width_x)
    faces_x = [
        (pl.ds(0, 4), end_x, all_z, 1, all_z, (right, gz)),
        (4, end_x, pl.ds(TOP + 1, width_z - 1), 1, pl.ds(TOP + 1, width_z - 1), (right, gz)),
        (5, end_x, pl.ds(TOP, width_z - 1), 1, pl.ds(TOP, width_z - 1), (right, gz)),
        (pl.ds(6, 4), 0, all_z, width_x, all_z, (left, gz)),
        (10, 0, pl.ds(TOP, width_z - 1), width_x, pl.ds(TOP, width_z - 1), (left, gz)),
        (11, 0, pl.ds(TOP + 1, width_z - 1), width_x, pl.ds(TOP + 1, width_z - 1), (left, gz)),
        (4, end_x, pl.ds(end_z, 1), 1, pl.ds(TOP, 1), (right, up)),
        (5, end_x, pl.ds(TOP - 1, 1), 1, pl.ds(end_z - 1, 1), (right, down)),
        (10, 0, pl.ds(TOP - 1, 1), width_x, pl.ds(end_z - 1, 1), (left, down)),
        (11, 0, pl.ds(end_z, 1), width_x, pl.ds(TOP, 1), (left, up)),
    ]
    late_x, early_x = pl.ds(2, width_x - 1), pl.ds(1, width_x - 1)
    faces_z = [
        (pl.ds(12, 4), all_x, pl.ds(end_z, 1), all_x, pl.ds(TOP, 1), (gx, up)),
        (4, late_x, pl.ds(end_z, 1), late_x, pl.ds(TOP, 1), (gx, up)),
        (11, early_x, pl.ds(end_z, 1), early_x, pl.ds(TOP, 1), (gx, up)),
        (pl.ds(16, 4), all_x, pl.ds(TOP - 1, 1), all_x, pl.ds(end_z - 1, 1), (gx, down)),
        (10, early_x, pl.ds(TOP - 1, 1), early_x, pl.ds(end_z - 1, 1), (gx, down)),
        (5, late_x, pl.ds(TOP - 1, 1), late_x, pl.ds(end_z - 1, 1), (gx, down)),
    ]

    def halo(t, which):
        copies = []
        for j, face in enumerate(faces_x + faces_z):
            if (j < len(faces_x)) != (which == 0):
                continue
            k, x_from, z_from, x_to, z_to, to = face
            copies.append(
                pltpu.make_async_remote_copy(
                    src_ref=states[t + 1].at[k, x_from, z_from, :],
                    dst_ref=states[t + 1].at[k, x_to, z_to, :],
                    send_sem=halo_ss.at[16 * t + j],
                    recv_sem=halo_rs.at[16 * t + j],
                    device_id=to,
                    device_id_type=MESH,
                )
            )
        return copies

    def step_flow(t):
        def ends(i, carry):
            collide(t, i * (width_x - 1))
            return carry

        def inner(x, carry):
            collide(t, x)
            return carry

        lax.fori_loop(0, 2, ends, 0)
        first = halo(t, 0)
        for copy in first:
            copy.start()
        lax.fori_loop(1, width_x - 1, inner, 0)
        second = halo(t, 1)
        for copy in second:
            copy.start()
        return first + second

    def grow(t, returned):
        high, low = zip(*[halves(returned(s)) for s in range(2)])
        there = product(disp_t[t], jnp.concatenate(high + low, axis=0))
        now = solid[...]
        solid[...] = now + caps[t] * there * (1.0 - now)

    def pack_rows(t, target):
        rows = packed(t)
        target[:, 0, :] = rows[0:n_dev]
        target[:, 1, :] = rows[n_dev : 2 * n_dev]

    def fill_back(t, target):
        rows = gather_mx(t)
        target[:, 0, :] = rows[0:n_dev]
        target[:, 1, :] = rows[n_dev : 2 * n_dev]

    for copy in loads:
        copy.wait()
    all_moments(0)
    drags[...] = jnp.zeros(drags.shape, F32)
    rows_here(0, out0_r)
    make_picks(0)
    fill_back(0, back0_s)
    send_rows(1, back0_s, back0_r)
    make_cover(0)
    halo0 = step_flow(0)
    gather_speed(0)
    make_drag(0)
    make_picks(1)
    make_picks(2)
    rows_here(1, back0_r)
    grow(0, lambda s: back0_r[:, s, :])
    pack_rows(1, out1_s)
    send_rows(2, out1_s, out1_r)

    for copy in halo0:
        copy.wait_recv()
    all_moments(1)
    fill_back(1, back1_s)
    send_rows(3, back1_s, back1_r)
    gather_speed(1)
    rows_here(2, out1_r)
    make_cover(1)
    halo1 = step_flow(1)
    make_drag(1)
    rows_here(3, back1_r)
    grow(1, lambda s: back1_r[:, s, :])
    pack_rows(2, out2_s)
    send_rows(4, out2_s, out2_r)

    for copy in halo1:
        copy.wait_recv()
    all_moments(2)
    rows = gather_mx(2)
    back2_s[:, 0, 0:128] = rows[0:n_dev]
    back2_s[:, 0, 128:256] = rows[n_dev : 2 * n_dev]
    gather_speed(2)
    rows_here(4, out2_r)
    make_drag(2)
    back2_s[:, 0, 256:384] = drags[...]
    send_rows(5, back2_s, back2_r)
    make_cover(2)
    halo2 = step_flow(2)
    for copy in halo2:
        copy.wait_recv()
    stores = []
    for k in range(26):
        goal = flow_out.at[k] if k < 19 else heat_out.at[k - 19]
        stores.append(
            pltpu.make_async_copy(
                w3.at[PLACE[k], pl.ds(1, width_x), pl.ds(TOP, width_z), :], goal, out_sem.at[k]
            )
        )
        stores[-1].start()
    rows_here(5, back2_r)
    grow(2, lambda s: back2_r[:, 0, s * 128 : (s + 1) * 128])
    solid_out[...] = solid[...]
    means = back2_r[:, 0, 256:384].T
    total = jnp.zeros((8, grains), F32)
    for t in range(3):
        for s in range(2):
            at = 8 * (2 * t + s)
            high, low = halves(means[at : at + 8, :])
            d = disp[t, s * n_dev : (s + 1) * n_dev, 0:grains]
            total = total + product(high, d) + product(low, d)
    drag_out[...] = total[0:3, :] * DRAG_SCALE

    for copy in halo0 + halo1 + halo2:
        copy.wait_send()
    for which, source in enumerate((out0_s, back0_s, out1_s, back1_s, out2_s, back2_s)):
        rows_sent(which, source)
    for copy in stores:
        copy.wait()


def on_device(sizes, populations, thermal, solid_blocks, centre_dev, centre_col, grain_velocity, capture):
    n_dev = sizes[0] * sizes[1]
    width_x, width_z, width_y = populations.shape[1:]
    grains = solid_blocks.shape[0]
    cells = width_x * width_z
    any_ = pl.BlockSpec(memory_space=pl.ANY)
    vmem = pl.BlockSpec(memory_space=pltpu.VMEM)
    state = pltpu.VMEM((26, width_x + 2, width_z + 16, width_y), F32)
    wide = pltpu.VMEM((n_dev, 1, 384), F32)
    plain = pltpu.VMEM((n_dev, 2, 128), F32)
    plane = (width_x, width_z, width_y)
    return pl.pallas_call(
        functools.partial(kernel, sizes),
        out_shape=(
            jax.ShapeDtypeStruct(populations.shape, F32),
            jax.ShapeDtypeStruct(thermal.shape, F32),
            jax.ShapeDtypeStruct(solid_blocks.shape, F32),
            jax.ShapeDtypeStruct((3, grains), F32),
        ),
        in_specs=[any_, any_, vmem, vmem, vmem, vmem, vmem],
        out_specs=(any_, any_, vmem, vmem),
        scratch_shapes=[
            state, state, state, state,
            pltpu.VMEM(plane, F32),
            pltpu.VMEM((3,) + plane, F32),
            pltpu.VMEM(plane, F32),
            pltpu.VMEM((2 * width_x, width_z, 128), BF16),
            pltpu.VMEM((2 * width_x, width_z, 384), BF16),
            pltpu.VMEM((width_x, width_z, 640), F32),
            pltpu.VMEM((128, grains), F32),
            pltpu.VMEM((3, 2 * n_dev, 2 * cells), BF16),
            pltpu.VMEM((3, cells, 4 * n_dev), BF16),
            pltpu.VMEM((3, 2 * n_dev, 2 * grains), BF16),
            pltpu.VMEM((3, grains, 4 * n_dev), BF16),
            pltpu.VMEM((3, grains, 128), F32),
            pltpu.VMEM((4 * n_dev, 640), BF16),
            pltpu.VMEM((grains, 128), F32),
            pltpu.VMEM((n_dev, 128), F32),
            pltpu.VMEM((2 * n_dev, 384), F32),
            wide, wide, plain, plain, plain, plain,
            plain, plain, plain, plain, wide, wide,
            pltpu.SemaphoreType.DMA((26,)),
            pltpu.SemaphoreType.DMA((26,)),
            pltpu.SemaphoreType.DMA((48,)),
            pltpu.SemaphoreType.DMA((48,)),
            pltpu.SemaphoreType.DMA((6,)),
            pltpu.SemaphoreType.DMA((6,)),
        ],
        compiler_params=pltpu.CompilerParams(
            collective_id=0, has_side_effects=True, vmem_limit_bytes=56 * 1024 * 1024
        ),
    )(
        populations,
        thermal,
        solid_blocks,
        centre_dev.reshape(3, grains),
        centre_col,
        grain_velocity.reshape(9, grains),
        capture,
    )


def solution(mesh):
    sizes = (mesh.shape["gx"], mesh.shape["gz"])
    placed = (
        P(None, "gx", "gz", None),
        P(None, "gx", "gz", None),
        P(("gx", "gz"), None),
        P(None, ("gx", "gz"), None),
        P(None, ("gx", "gz")),
        P(None, None, ("gx", "gz")),
        P(None, ("gx", "gz")),
    )
    return jax.shard_map(
        functools.partial(on_device, sizes),
        mesh=mesh,
        in_specs=placed,
        out_specs=(
            P(None, "gx", "gz", None),
            P(None, "gx", "gz", None),
            P(("gx", "gz"), None),
            P(None, ("gx", "gz")),
        ),
        check_vma=False,
    )
```

profile of v0, /device:TPU:1, one launch (start us, length us, event | category | flops | bytes accessed | tf_op | source)
XLA Modules:
  0.0 67.6 jit_solution(13914270826961760655)
XLA Ops:
  0.6 1.3 %copy.13 = s32[3,128,1]{1,0,2:T(4,128)} copy(s32[3,128,1]{1,2,0:T(1,128)} %param.10) | data formatting | bytes 3072
  1.9 1.3 %reshape.15.gvel = s32[9,128]{1,0:T(8,128)} reshape(s32[3,3,128]{2,1,0:T(4,128)} %param.12) | data formatting | bytes 9216 | tf_op jit(solution)/shard_map/reshape | solution.py:530
  3.2 58.6 %shard_map.102 = (f32[19,8,32,128]{3,2,1,0:T(8,128)}, f32[7,8,32,128]{3,2,1,0:T(8,128)}, f32[128,128]{1,0:T(8,128)}, f32[3,128]{1,0:T(4,128)}) custom-call(f32[19,8,32,128]{3,2,1,0:T(8,128)} %pop.1, f32[7,8,32,128]{3,2,1,0:T(8,128)} %th.1, f32[128,128]{1,0:T(8,128)} %solid_in.1, s32[3,128]{1,0:T(4,128)} %bitcast.3, s32[3,128]{1,0:T(4,128)} %ccol.1, ...), custom_call_target="tpu_custom_call" | custom-call | tf_op jit(solution)/shard_map/pallas_call | solution.py:484
  61.8 0.0 copy-start
  61.8 0.0 copy-start.1
  61.9 0.0 copy-start.2
  61.9 3.6 %copy.18 = f32[19,8,32,128]{3,2,1,0:T(8,128)} copy(f32[19,8,32,128]{3,2,1,0:T(8,128)} %get-tuple-element.8) | data formatting | bytes 4980736
  65.4 0.0 copy-done
  65.4 0.9 %copy.19 = f32[7,8,32,128]{3,2,1,0:T(8,128)} copy(f32[7,8,32,128]{3,2,1,0:T(8,128)S(1)} %copy-done) | data formatting | bytes 1835008
  66.3 0.0 copy-done.1
  66.3 0.6 copy.20
  67.0 0.0 copy-done.2
  67.0 0.6 copy.21
Async XLA Ops:
  61.8 3.6 %copy-start = (f32[7,8,32,128]{3,2,1,0:T(8,128)S(1)}, f32[7,8,32,128]{3,2,1,0:T(8,128)}, u32[]{:S(2)}) copy-start(f32[7,8,32,128]{3,2,1,0:T(8,128)} %get-tuple-element.9) | copy-start | bytes 2752516
  61.8 4.5 %copy-start.1 = (f32[128,128]{1,0:T(8,128)S(1)}, f32[128,128]{1,0:T(8,128)}, u32[]{:S(2)}) copy-start(f32[128,128]{1,0:T(8,128)} %get-tuple-element.10) | copy-start | bytes 196612
  61.9 5.1 %copy-start.2 = (f32[3,128]{1,0:T(4,128)S(1)}, f32[3,128]{1,0:T(4,128)}, u32[]{:S(2)}) copy-start(f32[3,128]{1,0:T(4,128)} %get-tuple-element.11) | copy-start | bytes 4612
where the time goes:
time: 67.8 us; the launch traced here: 67.6 us
  Pallas kernels  58.6 us (86%)
  local copies, waits for them, and re-layouts  8.25 us (12%)
    pallas_call x1, Pallas kernels, on_device(): pl.pallas_call(functools.partial(kernel, sizes), out_shape=(jax.ShapeDtyp...  58.6 us
    unnamed x11, local copies, waits for them, and re-layouts  6.96 us

commit v1 on v0

--- a/solution.py
+++ b/solution.py
@@ -62,13 +62,13 @@
 
 def kernel(
     sizes,
-    pop, th, solid_in, cdev, ccol, gvel, cap,
-    flow_out, heat_out, solid_out, drag_out,
-    w0, w1, w2, w3, dens, speeds, temps, mx_b, speed_b, cover,
+    pop, th, solid_in, cdev_in, ccol_in, gvel_in, cap_in,
+    w3, solid_out, drag_out,
+    w0, w1, w2, cdev, ccol, gvel, cap, dens, speeds, temps, mx_b, speed_b, cover,
     table, pick, pick_t, disp, disp_t, caps, spread, solid, drags, gathered,
     out0_s, out0_r, out1_s, out1_r, out2_s, out2_r,
-    back0_s, back0_r, back1_s, back1_r, back2_s, back2_r,
-    in_sem, out_sem, halo_ss, halo_rs, grain_ss, grain_rs,
+    back0_s, back0_r, back1_s, back1_r, back2_s, back2_r, drag_s, drag_r,
+    in_sem, halo_ss, halo_rs, grain_ss, grain_rs,
 ):
     n_gx, n_gz = sizes
     n_dev = n_gx * n_gz
@@ -78,17 +78,24 @@
     width_x, width_z = dens.shape[0], dens.shape[1]
     grains = solid.shape[0]
 
+    far = n_gx // 4
+    at_y = [lax.rem(gx // 4 + d, far) * 4 for d in range(far)]
+    at_x = [lax.rem(lax.rem(gx, 4) + d, 4) for d in range(4)]
+    at_z = [lax.rem(gz // 2 + d, n_gz // 2) * 2 for d in range(n_gz // 2)]
+    at_core = [lax.rem(gz, 2), 1 - lax.rem(gz, 2)]
+    by_gx = {(y, x): at_y[y] + at_x[x] for y in range(far) for x in range(4)}
+    by_gz = {(z, c): at_z[z] + at_core[c] for z in range(n_gz // 2) for c in range(2)}
+    apart = [(a, b) for a in by_gx for b in by_gz][1:]
+
+    def hops(pair):
+        (y, x), (z, c) = pair
+        return min(y, far - y) + min(x, 4 - x) + min(z, n_gz // 2 - z) + 0.5 * c
+
+    apart.sort(key=hops, reverse=True)
+
     def peers(body):
-        def group(i, carry):
-            k = 1 + lax.rem(n_gx // 2 + 1 + i, n_gx - 1)
-            there = lax.rem(gx + k, n_gx)
-            for d in (4, 3, 5, 2, 6, 1, 7, 0):
-                body(there, lax.rem(gz + d, n_gz))
-            return carry
-
-        lax.fori_loop(0, n_gx - 1, group, 0)
-        for d in (4, 3, 5, 2, 6, 1, 7):
-            body(gx, lax.rem(gz + d, n_gz))
+        for a, b in apart:
+            body(by_gx[a], by_gz[b])
 
     barrier = pltpu.get_barrier_semaphore()
     peers(lambda x, z: pl.semaphore_signal(barrier, inc=1, device_id=(x, z), device_id_type=MESH))
@@ -101,7 +108,13 @@
                 source, w0.at[PLACE[k], pl.ds(1, width_x), pl.ds(TOP, width_z), :], in_sem.at[k]
             )
         )
-        loads[-1].start()
+    small = []
+    for j, (source, goal) in enumerate(
+        ((cdev_in, cdev), (ccol_in, ccol), (gvel_in, gvel), (cap_in, cap), (solid_in, solid))
+    ):
+        small.append(pltpu.make_async_copy(source, goal, in_sem.at[26 + j]))
+    for copy in small + loads:
+        copy.start()
 
     def send_rows(which, source, target):
         def one(x, z):
@@ -125,6 +138,8 @@
         part = target.at[pl.ds(0, n_dev - 1)]
         pltpu.make_async_copy(part, part, grain_rs.at[which]).wait()
 
+    for copy in small:
+        copy.wait()
     square = (grains, grains)
     lane, row = lanes_of(square), rows_of(square)
     table[...] = jnp.zeros(table.shape, F32)
@@ -132,12 +147,12 @@
         table[8 * t : 8 * t + 1, :] = ccol[t : t + 1, :].astype(F32)
         table[8 * t + 1 : 8 * t + 2, :] = cap[t : t + 1, :].astype(F32)
         for c in range(3):
-            table[8 * t + 2 + c : 8 * t + 3 + c, :] = gvel[3 * t + c : 3 * t + c + 1, :].astype(F32)
+            table[8 * t + 2 + c : 8 * t + 3 + c, :] = gvel[t, c : c + 1, :].astype(F32)
     facts = table[...].T
     facts_moved = pltpu.roll(facts, grains // 2, axis=1)
     details = jnp.zeros((n_dev, grains), F32)
     for t in range(3):
-        goal = jnp.broadcast_to(cdev[t : t + 1, :].astype(F32), square)
+        goal = jnp.broadcast_to(cdev[t].astype(F32), square)
         goal_t = goal.T
         same = goal == goal_t
         rank = jnp.sum(chosen(same & (row < lane)), axis=0, keepdims=True)
@@ -161,7 +176,6 @@
         high, low = halves(solid[...])
         return product(disp[t], jnp.concatenate([high, low], axis=0))
 
-    solid[...] = solid_in[...]
     rows = packed(0)
     out0_s[:, 0, 0:128] = rows[0:n_dev]
     out0_s[:, 0, 128:256] = rows[n_dev : 2 * n_dev]
@@ -203,24 +217,36 @@
         mx_b[x] = high
         mx_b[width_x + x] = low
 
-    def all_moments(t):
+    def inner_moments(t):
         def one(x, carry):
             moments(t, x)
             return carry
 
-        lax.fori_loop(0, width_x, one, 0)
+        lax.fori_loop(1, width_x - 1, one, 0)
+
+    def outer_moments(t):
+        def one(i, carry):
+            moments(t, i * (width_x - 1))
+            return carry
+
+        lax.fori_loop(0, 2, one, 0)
 
     cells = width_x * width_z
 
-    def make_picks(t):
+    def make_pick(t):
         detail = out0_r[:, 0, 256:384]
-        detail_t = detail.T
         for s in range(2):
             at = 64 * s + 8 * t
             p = chosen(lanes_of((n_dev, cells)) == detail[:, at : at + 1]).astype(BF16)
+            for half in range(2):
+                pick[t, s * n_dev : (s + 1) * n_dev, half * cells : (half + 1) * cells] = p
+
+    def make_pick_t(t):
+        detail_t = out0_r[:, 0, 256:384].T
+        for s in range(2):
+            at = 64 * s + 8 * t
             p_t = chosen(rows_of((cells, n_dev)) == detail_t[at : at + 1, :]).astype(BF16)
             for half in range(2):
-                pick[t, s * n_dev : (s + 1) * n_dev, half * cells : (half + 1) * cells] = p
                 k = (2 * half + s) * n_dev
                 pick_t[t, :, k : k + n_dev] = p_t
 
@@ -232,7 +258,7 @@
             return out0_r[:, 0, s * 128 : (s + 1) * 128]
         return (out1_r if t == 1 else out2_r)[:, s, :]
 
-    def make_cover(t):
+    def make_spread(t):
         detail = out0_r[:, 0, 256:384]
         for s in range(2):
             block = blocks_here(t, s)
@@ -245,24 +271,36 @@
                 high, low = halves(parts[c])
                 spread[s * n_dev : (s + 1) * n_dev, c * 128 : (c + 1) * 128] = high
                 spread[(2 + s) * n_dev : (3 + s) * n_dev, c * 128 : (c + 1) * 128] = low
-        cover[...] = product(pick_t[t], spread[...]).reshape(width_x, width_z, 640)
+
+    def outer_cover(t):
+        rows = product(
+            jnp.concatenate([pick_t[t, 0:width_z], pick_t[t, cells - width_z : cells]], axis=0),
+            spread[...],
+        )
+        cover[0] = rows[0:width_z]
+        cover[width_x - 1] = rows[width_z : 2 * width_z]
+
+    def inner_cover(t):
+        rows = product(pick_t[t, width_z : cells - width_z], spread[...])
+        cover[1 : width_x - 1] = rows.reshape(width_x - 2, width_z, 640)
 
     def gather_speed(t):
         gathered[...] = product(pick[t], speed_b[...].reshape(2 * cells, 384))
 
     def make_drag(t):
         detail = out0_r[:, 0, 256:384]
-        lane_d = lanes_of((n_dev, 128))
-        total = drags[...]
+        parts, marks = [], []
         for s in range(2):
             block = blocks_here(t, s)
             at = 64 * s + 8 * t
             for c in range(3):
                 speed = gathered[s * n_dev : (s + 1) * n_dev, c * 128 : (c + 1) * 128]
                 drag = block * (speed - detail[:, at + 2 + c : at + 3 + c] * VEL_UNIT)
-                mean = jnp.sum(drag, axis=1, keepdims=True) * (BETA / 128.0)
-                total = jnp.where(lane_d == 8 * (2 * t + s) + c, mean, total)
-        drags[...] = total
+                parts.extend(halves(drag))
+                mark = chosen(lanes_of((128, 128)) == 8 * (2 * t + s) + c).astype(BF16)
+                marks.extend((mark, mark))
+        total = product(jnp.concatenate(parts, axis=1), jnp.concatenate(marks, axis=0))
+        drags[...] = drags[...] + total * (BETA / 128.0)
 
     def collide(t, x):
         w, after = states[t], states[t + 1]
@@ -356,24 +394,29 @@
             )
         return copies
 
-    def step_flow(t):
+    def outer_flow(t):
         def ends(i, carry):
             collide(t, i * (width_x - 1))
             return carry
 
+        outer_cover(t)
+        lax.fori_loop(0, 2, ends, 0)
+        copies = halo(t, 0)
+        for copy in copies:
+            copy.start()
+        return copies
+
+    def inner_flow(t):
         def inner(x, carry):
             collide(t, x)
             return carry
 
-        lax.fori_loop(0, 2, ends, 0)
-        first = halo(t, 0)
-        for copy in first:
+        inner_cover(t)
+        lax.fori_loop(1, width_x - 1, inner, 0)
+        copies = halo(t, 1)
+        for copy in copies:
             copy.start()
-        lax.fori_loop(1, width_x - 1, inner, 0)
-        second = halo(t, 1)
-        for copy in second:
-            copy.start()
-        return first + second
+        return copies
 
     def grow(t, returned):
         high, low = zip(*[halves(returned(s)) for s in range(2)])
@@ -393,66 +436,68 @@
 
     for copy in loads:
         copy.wait()
-    all_moments(0)
+    outer_moments(0)
+    inner_moments(0)
     drags[...] = jnp.zeros(drags.shape, F32)
     rows_here(0, out0_r)
-    make_picks(0)
+    make_pick(0)
     fill_back(0, back0_s)
     send_rows(1, back0_s, back0_r)
-    make_cover(0)
-    halo0 = step_flow(0)
+    make_pick_t(0)
+    make_spread(0)
+    x0 = outer_flow(0)
+    z0 = inner_flow(0)
+    make_pick(1)
+    make_pick_t(1)
     gather_speed(0)
     make_drag(0)
-    make_picks(1)
-    make_picks(2)
+    make_pick(2)
+    make_pick_t(2)
+    for copy in z0:
+        copy.wait_recv()
+    inner_moments(1)
     rows_here(1, back0_r)
     grow(0, lambda s: back0_r[:, s, :])
     pack_rows(1, out1_s)
     send_rows(2, out1_s, out1_r)
 
-    for copy in halo0:
+    for copy in x0:
         copy.wait_recv()
-    all_moments(1)
+    outer_moments(1)
     fill_back(1, back1_s)
     send_rows(3, back1_s, back1_r)
     gather_speed(1)
     rows_here(2, out1_r)
-    make_cover(1)
-    halo1 = step_flow(1)
-    make_drag(1)
+    make_spread(1)
+    x1 = outer_flow(1)
     rows_here(3, back1_r)
     grow(1, lambda s: back1_r[:, s, :])
     pack_rows(2, out2_s)
     send_rows(4, out2_s, out2_r)
-
-    for copy in halo1:
+    z1 = inner_flow(1)
+    make_drag(1)
+
+    for copy in z1:
         copy.wait_recv()
-    all_moments(2)
-    rows = gather_mx(2)
-    back2_s[:, 0, 0:128] = rows[0:n_dev]
-    back2_s[:, 0, 128:256] = rows[n_dev : 2 * n_dev]
+    inner_moments(2)
+    for copy in x1:
+        copy.wait_recv()
+    outer_moments(2)
+    fill_back(2, back2_s)
+    send_rows(5, back2_s, back2_r)
     gather_speed(2)
     rows_here(4, out2_r)
     make_drag(2)
-    back2_s[:, 0, 256:384] = drags[...]
-    send_rows(5, back2_s, back2_r)
-    make_cover(2)
-    halo2 = step_flow(2)
-    for copy in halo2:
-        copy.wait_recv()
-    stores = []
-    for k in range(26):
-        goal = flow_out.at[k] if k < 19 else heat_out.at[k - 19]
-        stores.append(
-            pltpu.make_async_copy(
-                w3.at[PLACE[k], pl.ds(1, width_x), pl.ds(TOP, width_z), :], goal, out_sem.at[k]
-            )
-        )
-        stores[-1].start()
+    drag_s[:, 0, :] = drags[...]
+    send_rows(6, drag_s, drag_r)
+    make_spread(2)
+    x2 = outer_flow(2)
+    z2 = inner_flow(2)
     rows_here(5, back2_r)
-    grow(2, lambda s: back2_r[:, 0, s * 128 : (s + 1) * 128])
+    grow(2, lambda s: back2_r[:, s, :])
     solid_out[...] = solid[...]
-    means = back2_r[:, 0, 256:384].T
+    rows_here(6, drag_r)
+    means = drag_r[:, 0, :].T
     total = jnp.zeros((8, grains), F32)
     for t in range(3):
         for s in range(2):
@@ -462,11 +507,28 @@
             total = total + product(high, d) + product(low, d)
     drag_out[...] = total[0:3, :] * DRAG_SCALE
 
-    for copy in halo0 + halo1 + halo2:
+    for copy in z2 + x2:
+        copy.wait_recv()
+    for copy in z0 + x0 + z1 + x1 + z2 + x2:
         copy.wait_send()
-    for which, source in enumerate((out0_s, back0_s, out1_s, back1_s, out2_s, back2_s)):
+    sources = (out0_s, back0_s, out1_s, back1_s, out2_s, back2_s, drag_s)
+    for which, source in enumerate(sources):
         rows_sent(which, source)
-    for copy in stores:
+
+
+def deliver(state, solid, drag, flow_out, heat_out, solid_out, drag_out, sem):
+    width_x, width_z = flow_out.shape[1], flow_out.shape[2]
+    copies = [
+        pltpu.make_async_copy(solid, solid_out, sem.at[26]),
+        pltpu.make_async_copy(drag, drag_out, sem.at[27]),
+    ]
+    for k in range(26):
+        goal = flow_out.at[k] if k < 19 else heat_out.at[k - 19]
+        source = state.at[PLACE[k], pl.ds(1, width_x), pl.ds(TOP, width_z), :]
+        copies.append(pltpu.make_async_copy(source, goal, sem.at[k]))
+    for copy in copies:
+        copy.start()
+    for copy in copies:
         copy.wait()
 
 
@@ -475,24 +537,37 @@
     width_x, width_z, width_y = populations.shape[1:]
     grains = solid_blocks.shape[0]
     cells = width_x * width_z
-    any_ = pl.BlockSpec(memory_space=pl.ANY)
     vmem = pl.BlockSpec(memory_space=pltpu.VMEM)
     state = pltpu.VMEM((26, width_x + 2, width_z + 16, width_y), F32)
     wide = pltpu.VMEM((n_dev, 1, 384), F32)
     plain = pltpu.VMEM((n_dev, 2, 128), F32)
+    thin = pltpu.VMEM((n_dev, 1, 128), F32)
     plane = (width_x, width_z, width_y)
-    return pl.pallas_call(
+    hbm = pl.BlockSpec(memory_space=pltpu.HBM)
+    operands = (
+        populations,
+        thermal,
+        solid_blocks,
+        jnp.swapaxes(centre_dev, 1, 2),
+        centre_col,
+        grain_velocity,
+        capture,
+    )
+    after, solid, drag = pl.pallas_call(
         functools.partial(kernel, sizes),
         out_shape=(
-            jax.ShapeDtypeStruct(populations.shape, F32),
-            jax.ShapeDtypeStruct(thermal.shape, F32),
-            jax.ShapeDtypeStruct(solid_blocks.shape, F32),
-            jax.ShapeDtypeStruct((3, grains), F32),
+            state,
+            pltpu.VMEM(solid_blocks.shape, F32),
+            pltpu.VMEM((3, grains), F32),
         ),
-        in_specs=[any_, any_, vmem, vmem, vmem, vmem, vmem],
-        out_specs=(any_, any_, vmem, vmem),
+        in_specs=[hbm] * 7,
+        out_specs=(vmem, vmem, vmem),
         scratch_shapes=[
-            state, state, state, state,
+            state, state, state,
+            pltpu.VMEM((3, 1, grains), jnp.int32),
+            pltpu.VMEM((3, grains), jnp.int32),
+            pltpu.VMEM((3, 3, grains), jnp.int32),
+            pltpu.VMEM((3, grains), jnp.int32),
             pltpu.VMEM(plane, F32),
             pltpu.VMEM((3,) + plane, F32),
             pltpu.VMEM(plane, F32),
@@ -510,26 +585,30 @@
             pltpu.VMEM((n_dev, 128), F32),
             pltpu.VMEM((2 * n_dev, 384), F32),
             wide, wide, plain, plain, plain, plain,
-            plain, plain, plain, plain, wide, wide,
-            pltpu.SemaphoreType.DMA((26,)),
-            pltpu.SemaphoreType.DMA((26,)),
+            plain, plain, plain, plain, plain, plain, thin, thin,
+            pltpu.SemaphoreType.DMA((31,)),
             pltpu.SemaphoreType.DMA((48,)),
             pltpu.SemaphoreType.DMA((48,)),
-            pltpu.SemaphoreType.DMA((6,)),
-            pltpu.SemaphoreType.DMA((6,)),
+            pltpu.SemaphoreType.DMA((7,)),
+            pltpu.SemaphoreType.DMA((7,)),
         ],
         compiler_params=pltpu.CompilerParams(
-            collective_id=0, has_side_effects=True, vmem_limit_bytes=56 * 1024 * 1024
+            collective_id=0, has_side_effects=True, vmem_limit_bytes=50 * 1024 * 1024
         ),
-    )(
-        populations,
-        thermal,
-        solid_blocks,
-        centre_dev.reshape(3, grains),
-        centre_col,
-        grain_velocity.reshape(9, grains),
-        capture,
-    )
+    )(*[pltpu.with_memory_space_constraint(given, pltpu.HBM) for given in operands])
+    return pl.pallas_call(
+        deliver,
+        out_shape=(
+            jax.ShapeDtypeStruct(populations.shape, F32),
+            jax.ShapeDtypeStruct(thermal.shape, F32),
+            jax.ShapeDtypeStruct(solid_blocks.shape, F32),
+            jax.ShapeDtypeStruct((3, grains), F32),
+        ),
+        in_specs=[vmem] * 3,
+        out_specs=[hbm] * 4,
+        scratch_shapes=[pltpu.SemaphoreType.DMA((28,))],
+        compiler_params=pltpu.CompilerParams(vmem_limit_bytes=1024 * 1024),
+    )(*[pltpu.with_memory_space_constraint(made, pltpu.VMEM) for made in (after, solid, drag)])
 
 
 def solution(mesh):

time: 67.8 us -> 56.6 us (0.83); the launches traced: 67.6 us -> 55.7 us
  local copies, waits for them, and re-layouts: 8.25 us -> 0 us
  Pallas kernels: 58.6 us -> 54.9 us
    unnamed x11 -> x0, local copies, waits for them, and re-layouts: 6.96 us -> none
    pallas_call x1 -> x2, Pallas kernels: 58.6 us -> 54.9 us  [the longest x1 52.9 us: on_device(): pl.pallas_call(functools.partial(kernel, sizes), out_shape=(state, pltpu....]
    reshape x1 -> x0, local copies, waits for them, and re-layouts: 1.3 us -> none  [on_device(): grain_velocity.reshape(9, grains)]
where the time goes in v1:
time: 56.6 us; the launch traced here: 55.7 us
  Pallas kernels  54.9 us (97%)
  between operations  0.8 us (1%)
    pallas_call x1, Pallas kernels, on_device(): pl.pallas_call(functools.partial(kernel, sizes), out_shape=(state, pltpu....  52.9 us
    pallas_call x1, Pallas kernels, on_device(): pl.pallas_call(deliver, out_shape=(jax.ShapeDtypeStruct(populations.shape...  2 us

profile of v1, /device:TPU:1, one launch (start us, length us, event | category | flops | bytes accessed | tf_op | source)
XLA Modules:
  0.0 55.7 jit_solution(17319929045491317221)
XLA Ops:
  0.6 52.9 %shard_map.102 = (f32[26,10,48,128]{3,2,1,0:T(8,128)S(1)}, f32[128,128]{1,0:T(8,128)S(1)}, f32[3,128]{1,0:T(4,128)S(1)}) custom-call(f32[19,8,32,128]{3,2,1,0:T(8,128)} %pop.1, f32[7,8,32,128]{3,2,1,0:T(8,128)} %th.1, f32[128,128]{1,0:T(8,128)} %solid_in.1, s32[3,1,128]{2,1,0:T(1,128)} %bitcast.1, s32[3,128]{1,0:T(4,128)} %ccol_in.1, s32[3,3,128]{2,1,0:T(4,128)} %gvel_in.1, ...), custom_call_target="tpu_custom_call" | custom-call | tf_op jit(solution)/shard_map/pallas_call | solution.py:556
  53.5 2.0 %shard_map.103 = (f32[19,8,32,128]{3,2,1,0:T(8,128)}, f32[7,8,32,128]{3,2,1,0:T(8,128)}, f32[128,128]{1,0:T(8,128)}, f32[3,128]{1,0:T(4,128)}) custom-call(f32[26,10,48,128]{3,2,1,0:T(8,128)S(1)} %get-tuple-element.7.state, f32[128,128]{1,0:T(8,128)S(1)} %get-tuple-element.8.solid, f32[3,128]{1,0:T(4,128)S(1)} %get-tuple-element.9.drag), custom_call_target="tpu_custom_call" | custom-call | tf_op jit(solution)/shard_map/pallas_call | solution.py:599

commit v2 on v1

--- a/solution.py
+++ b/solution.py
@@ -64,10 +64,10 @@
     sizes,
     pop, th, solid_in, cdev_in, ccol_in, gvel_in, cap_in,
     w3, solid_out, drag_out,
-    w0, w1, w2, cdev, ccol, gvel, cap, dens, speeds, temps, mx_b, speed_b, cover,
-    table, pick, pick_t, disp, disp_t, caps, spread, solid, drags, gathered,
+    w0, w1, w2, cdev, ccol, gvel, cap, dens, speeds, temps, mx_b, speed_b, cover, warmed,
+    table, pick, pick_t, disp, disp_t, caps, fast, taken, spread, spread_h, solid, drags, gathered,
     out0_s, out0_r, out1_s, out1_r, out2_s, out2_r,
-    back0_s, back0_r, back1_s, back1_r, back2_s, back2_r, drag_s, drag_r,
+    back0_s, back0_r, back1_s, back1_r, back2_s, back2_r,
     in_sem, halo_ss, halo_rs, grain_ss, grain_rs,
 ):
     n_gx, n_gz = sizes
@@ -184,7 +184,7 @@
     pl.semaphore_wait(barrier, n_dev - 1)
     send_rows(0, out0_s, out0_r)
 
-    def moments(t, x):
+    def flow_moments(t, x):
         w = states[t]
 
         def at(k):
@@ -201,11 +201,7 @@
                     momentum[c] = apart if momentum[c] is None else momentum[c] + apart
                 elif FLOW[a][c] == -1:
                     momentum[c] = momentum[c] - apart
-        temper = at(19)
-        for k in range(20, 26):
-            temper = temper + at(k)
         dens[x] = density
-        temps[x] = temper
         inverse = 1.0 / density
         for c in range(3):
             speed = momentum[c] * inverse
@@ -213,23 +209,33 @@
             high, low = halves(speed)
             speed_b[x, :, c * 128 : (c + 1) * 128] = high
             speed_b[width_x + x, :, c * 128 : (c + 1) * 128] = low
+
+    def heat_moments(t, x):
+        w = states[t]
+        parts = [w[PLACE[k], x + 1, TOP : TOP + width_z, :] for k in range(19, 26)]
+        temper = parts[0]
+        for part in parts[1:]:
+            temper = temper + part
+        temps[t % 2, x] = temper
         high, low = halves(jnp.maximum(1.0 - temper, 0.0))
         mx_b[x] = high
         mx_b[width_x + x] = low
 
+    def over(planes, first, step, body):
+        def one(i, carry):
+            body(first + i * step)
+            return carry
+
+        lax.fori_loop(0, planes, one, 0)
+
     def inner_moments(t):
-        def one(x, carry):
-            moments(t, x)
-            return carry
-
-        lax.fori_loop(1, width_x - 1, one, 0)
+        over(width_x - 2, 1, 1, lambda x: flow_moments(t, x))
 
     def outer_moments(t):
-        def one(i, carry):
-            moments(t, i * (width_x - 1))
-            return carry
-
-        lax.fori_loop(0, 2, one, 0)
+        over(2, 0, width_x - 1, lambda x: flow_moments(t, x))
+
+    def all_heat_moments(t):
+        over(width_x, 0, 1, lambda x: heat_moments(t, x))
 
     cells = width_x * width_z
 
@@ -258,19 +264,31 @@
             return out0_r[:, 0, s * 128 : (s + 1) * 128]
         return (out1_r if t == 1 else out2_r)[:, s, :]
 
+    def make_facts(t):
+        detail = out0_r[:, 0, 256:384]
+        shape = (n_dev, 128)
+        for s in range(2):
+            at = 64 * s + 8 * t
+            taken[t, s] = jnp.broadcast_to(detail[:, at + 1 : at + 2], shape)
+            for c in range(3):
+                speed = detail[:, at + 2 + c : at + 3 + c] * VEL_UNIT
+                fast[t, s, c] = jnp.broadcast_to(speed, shape)
+
     def make_spread(t):
-        detail = out0_r[:, 0, 256:384]
         for s in range(2):
             block = blocks_here(t, s)
-            at = 64 * s + 8 * t
-            parts = [block]
-            for c in range(3):
-                parts.append(block * (detail[:, at + 2 + c : at + 3 + c] * VEL_UNIT))
-            parts.append(detail[:, at + 1 : at + 2] * (1.0 - block))
-            for c in range(5):
+            parts = [block] + [block * fast[t, s, c] for c in range(3)]
+            for c in range(4):
                 high, low = halves(parts[c])
                 spread[s * n_dev : (s + 1) * n_dev, c * 128 : (c + 1) * 128] = high
                 spread[(2 + s) * n_dev : (3 + s) * n_dev, c * 128 : (c + 1) * 128] = low
+
+    def heat_cover(t):
+        for s in range(2):
+            high, low = halves(taken[t, s] * (1.0 - blocks_here(t, s)))
+            spread_h[s * n_dev : (s + 1) * n_dev, :] = high
+            spread_h[(2 + s) * n_dev : (3 + s) * n_dev, :] = low
+        warmed[...] = product(pick_t[t], spread_h[...]).reshape(width_x, width_z, 128)
 
     def outer_cover(t):
         rows = product(
@@ -282,72 +300,74 @@
 
     def inner_cover(t):
         rows = product(pick_t[t, width_z : cells - width_z], spread[...])
-        cover[1 : width_x - 1] = rows.reshape(width_x - 2, width_z, 640)
+        cover[1 : width_x - 1] = rows.reshape(width_x - 2, width_z, 512)
 
     def gather_speed(t):
         gathered[...] = product(pick[t], speed_b[...].reshape(2 * cells, 384))
 
     def make_drag(t):
-        detail = out0_r[:, 0, 256:384]
         parts, marks = [], []
         for s in range(2):
             block = blocks_here(t, s)
-            at = 64 * s + 8 * t
             for c in range(3):
                 speed = gathered[s * n_dev : (s + 1) * n_dev, c * 128 : (c + 1) * 128]
-                drag = block * (speed - detail[:, at + 2 + c : at + 3 + c] * VEL_UNIT)
-                parts.extend(halves(drag))
+                parts.extend(halves(block * (speed - fast[t, s, c])))
                 mark = chosen(lanes_of((128, 128)) == 8 * (2 * t + s) + c).astype(BF16)
                 marks.extend((mark, mark))
         total = product(jnp.concatenate(parts, axis=1), jnp.concatenate(marks, axis=0))
         drags[...] = drags[...] + total * (BETA / 128.0)
 
-    def collide(t, x):
-        w, after = states[t], states[t + 1]
-        tall = 16
+    tall = 16
+
+    def put(t, x, z, k, value):
+        velo = FLOW[k] if k < 19 else HEAT[k - 19]
+        if velo[1]:
+            value = pltpu.roll(value, velo[1] % 128, axis=1)
+        start = TOP + z + velo[2]
+        states[t + 1][PLACE[k], x + 1 + velo[0], start : start + tall, :] = value
+
+    def at_cell(t, x, z, k):
+        return states[t][PLACE[k], x + 1, TOP + z : TOP + z + tall, :]
+
+    def collide_flow(t, x):
         for z in range(0, width_z, tall):
             here = slice(z, z + tall)
-
-            def put(k, value):
-                velo = FLOW[k] if k < 19 else HEAT[k - 19]
-                if velo[1]:
-                    value = pltpu.roll(value, velo[1] % 128, axis=1)
-                start = TOP + z + velo[2]
-                after[PLACE[k], x + 1 + velo[0], start : start + tall, :] = value
-
-            def at(k):
-                return w[PLACE[k], x + 1, TOP + z : TOP + z + tall, :]
-
+            put_, at = functools.partial(put, t, x, z), functools.partial(at_cell, t, x, z)
             density = dens[x, here, :]
-            temper = temps[x, here, :]
             speed = [speeds[c, x, here, :] for c in range(3)]
-            spots = [cover[x, here, c * 128 : (c + 1) * 128] for c in range(5)]
+            spots = [cover[x, here, c * 128 : (c + 1) * 128] for c in range(4)]
             pull = (TAU * BETA) / density
             shifted = [speed[c] + pull * (spots[1 + c] - spots[0] * speed[c]) for c in range(3)]
-            shifted[2] = shifted[2] + (TAU * BUOY) * (temper - 1.0)
+            shifted[2] = shifted[2] + (TAU * BUOY) * (temps[t % 2, x, here, :] - 1.0)
             square_ = shifted[0] * shifted[0] + shifted[1] * shifted[1] + shifted[2] * shifted[2]
             base18 = density * (1.0 / (18.0 * TAU)) * (1.0 - 1.5 * square_)
             base36 = 0.5 * base18
             way18 = density * (3.0 / (18.0 * TAU))
             way36 = 0.5 * way18
             keep = 1.0 - 1.0 / TAU
-            put(0, 6.0 * base18 + keep * at(0))
+            put_(0, 6.0 * base18 + keep * at(0))
             for a, b in PAIRS:
                 along = dotted(FLOW[a], shifted)
                 odd = (way18 if a < 7 else way36) * along
                 even = (base18 if a < 7 else base36) + 1.5 * along * odd
-                put(a, even + odd + keep * at(a))
-                put(b, even - odd + keep * at(b))
+                put_(a, even + odd + keep * at(a))
+                put_(b, even - odd + keep * at(b))
+
+    def collide_heat(t, x):
+        for z in range(0, width_z, tall):
+            here = slice(z, z + tall)
+            put_, at = functools.partial(put, t, x, z), functools.partial(at_cell, t, x, z)
+            temper = temps[t % 2, x, here, :]
             keep = 1.0 - 1.0 / TAU_T
-            latent = LATENT * jnp.maximum(1.0 - temper, 0.0) * spots[4]
+            latent = LATENT * jnp.maximum(1.0 - temper, 0.0) * warmed[x, here, :]
             warm = temper * (1.0 / TAU_T)
             even = 0.125 * (warm + latent)
-            put(19, 2.0 * even + keep * at(19))
+            put_(19, 2.0 * even + keep * at(19))
             half_warm = 0.5 * warm
-            for c, axis_id in ((0, 0), (1, 1), (2, 2)):
-                odd = half_warm * speed[axis_id]
-                put(20 + 2 * c, even + odd + keep * at(20 + 2 * c))
-                put(21 + 2 * c, even - odd + keep * at(21 + 2 * c))
+            for c in range(3):
+                odd = half_warm * speeds[c, x, here, :]
+                put_(20 + 2 * c, even + odd + keep * at(20 + 2 * c))
+                put_(21 + 2 * c, even - odd + keep * at(21 + 2 * c))
 
     left, right = lax.rem(gx + n_gx - 1, n_gx), lax.rem(gx + 1, n_gx)
     down, up = lax.rem(gz + n_gz - 1, n_gz), lax.rem(gz + 1, n_gz)
@@ -355,10 +375,10 @@
     all_z = pl.ds(TOP, width_z)
     all_x = pl.ds(1, width_x)
     faces_x = [
-        (pl.ds(0, 4), end_x, all_z, 1, all_z, (right, gz)),
+        (pl.ds(0, 3), end_x, all_z, 1, all_z, (right, gz)),
         (4, end_x, pl.ds(TOP + 1, width_z - 1), 1, pl.ds(TOP + 1, width_z - 1), (right, gz)),
         (5, end_x, pl.ds(TOP, width_z - 1), 1, pl.ds(TOP, width_z - 1), (right, gz)),
-        (pl.ds(6, 4), 0, all_z, width_x, all_z, (left, gz)),
+        (pl.ds(6, 3), 0, all_z, width_x, all_z, (left, gz)),
         (10, 0, pl.ds(TOP, width_z - 1), width_x, pl.ds(TOP, width_z - 1), (left, gz)),
         (11, 0, pl.ds(TOP + 1, width_z - 1), width_x, pl.ds(TOP + 1, width_z - 1), (left, gz)),
         (4, end_x, pl.ds(end_z, 1), 1, pl.ds(TOP, 1), (right, up)),
@@ -368,55 +388,52 @@
     ]
     late_x, early_x = pl.ds(2, width_x - 1), pl.ds(1, width_x - 1)
     faces_z = [
-        (pl.ds(12, 4), all_x, pl.ds(end_z, 1), all_x, pl.ds(TOP, 1), (gx, up)),
+        (pl.ds(12, 3), all_x, pl.ds(end_z, 1), all_x, pl.ds(TOP, 1), (gx, up)),
         (4, late_x, pl.ds(end_z, 1), late_x, pl.ds(TOP, 1), (gx, up)),
         (11, early_x, pl.ds(end_z, 1), early_x, pl.ds(TOP, 1), (gx, up)),
-        (pl.ds(16, 4), all_x, pl.ds(TOP - 1, 1), all_x, pl.ds(end_z - 1, 1), (gx, down)),
+        (pl.ds(16, 3), all_x, pl.ds(TOP - 1, 1), all_x, pl.ds(end_z - 1, 1), (gx, down)),
         (10, early_x, pl.ds(TOP - 1, 1), early_x, pl.ds(end_z - 1, 1), (gx, down)),
         (5, late_x, pl.ds(TOP - 1, 1), late_x, pl.ds(end_z - 1, 1), (gx, down)),
     ]
 
-    def halo(t, which):
+    faces_h = [
+        (3, end_x, all_z, 1, all_z, (right, gz)),
+        (9, 0, all_z, width_x, all_z, (left, gz)),
+        (15, all_x, pl.ds(end_z, 1), all_x, pl.ds(TOP, 1), (gx, up)),
+        (19, all_x, pl.ds(TOP - 1, 1), all_x, pl.ds(end_z - 1, 1), (gx, down)),
+    ]
+
+    def halo(t, first, faces):
         copies = []
-        for j, face in enumerate(faces_x + faces_z):
-            if (j < len(faces_x)) != (which == 0):
-                continue
-            k, x_from, z_from, x_to, z_to, to = face
+        for j, (k, x_from, z_from, x_to, z_to, to) in enumerate(faces):
             copies.append(
                 pltpu.make_async_remote_copy(
                     src_ref=states[t + 1].at[k, x_from, z_from, :],
                     dst_ref=states[t + 1].at[k, x_to, z_to, :],
-                    send_sem=halo_ss.at[16 * t + j],
-                    recv_sem=halo_rs.at[16 * t + j],
+                    send_sem=halo_ss.at[20 * t + first + j],
+                    recv_sem=halo_rs.at[20 * t + first + j],
                     device_id=to,
                     device_id_type=MESH,
                 )
             )
+            copies[-1].start()
         return copies
 
     def outer_flow(t):
-        def ends(i, carry):
-            collide(t, i * (width_x - 1))
-            return carry
-
-        outer_cover(t)
-        lax.fori_loop(0, 2, ends, 0)
-        copies = halo(t, 0)
+        over(2, 0, width_x - 1, lambda x: collide_flow(t, x))
+        return halo(t, 0, faces_x)
+
+    def inner_flow(t):
+        over(width_x - 2, 1, 1, lambda x: collide_flow(t, x))
+        return halo(t, 10, faces_z)
+
+    def heat(t):
+        over(width_x, 0, 1, lambda x: collide_heat(t, x))
+        return halo(t, 16, faces_h)
+
+    def landed(copies):
         for copy in copies:
-            copy.start()
-        return copies
-
-    def inner_flow(t):
-        def inner(x, carry):
-            collide(t, x)
-            return carry
-
-        inner_cover(t)
-        lax.fori_loop(1, width_x - 1, inner, 0)
-        copies = halo(t, 1)
-        for copy in copies:
-            copy.start()
-        return copies
+            copy.wait_recv()
 
     def grow(t, returned):
         high, low = zip(*[halves(returned(s)) for s in range(2)])
@@ -438,66 +455,82 @@
         copy.wait()
     outer_moments(0)
     inner_moments(0)
+    all_heat_moments(0)
     drags[...] = jnp.zeros(drags.shape, F32)
     rows_here(0, out0_r)
     make_pick(0)
     fill_back(0, back0_s)
     send_rows(1, back0_s, back0_r)
     make_pick_t(0)
+    make_facts(0)
+    heat_cover(0)
+    h0 = heat(0)
     make_spread(0)
+    outer_cover(0)
     x0 = outer_flow(0)
-    z0 = inner_flow(0)
     make_pick(1)
-    make_pick_t(1)
-    gather_speed(0)
-    make_drag(0)
-    make_pick(2)
-    make_pick_t(2)
-    for copy in z0:
-        copy.wait_recv()
-    inner_moments(1)
+    inner_cover(0)
+    landed(h0)
+    all_heat_moments(1)
+    fill_back(1, back1_s)
+    send_rows(3, back1_s, back1_r)
     rows_here(1, back0_r)
     grow(0, lambda s: back0_r[:, s, :])
     pack_rows(1, out1_s)
     send_rows(2, out1_s, out1_r)
-
-    for copy in x0:
-        copy.wait_recv()
+    z0 = inner_flow(0)
+    gather_speed(0)
+    make_drag(0)
+    make_pick_t(1)
+    make_facts(1)
+    make_pick(2)
+    make_pick_t(2)
+    make_facts(2)
+    landed(z0)
+    inner_moments(1)
+    landed(x0)
     outer_moments(1)
-    fill_back(1, back1_s)
-    send_rows(3, back1_s, back1_r)
     gather_speed(1)
-    rows_here(2, out1_r)
-    make_spread(1)
-    x1 = outer_flow(1)
+
     rows_here(3, back1_r)
     grow(1, lambda s: back1_r[:, s, :])
     pack_rows(2, out2_s)
     send_rows(4, out2_s, out2_r)
+    rows_here(2, out1_r)
+    make_spread(1)
+    outer_cover(1)
+    x1 = outer_flow(1)
+    heat_cover(1)
+    h1 = heat(1)
+    inner_cover(1)
     z1 = inner_flow(1)
     make_drag(1)
-
-    for copy in z1:
-        copy.wait_recv()
+    rows_here(4, out2_r)
+    make_spread(2)
+    outer_cover(2)
+    inner_cover(2)
+    heat_cover(2)
+
+    landed(h1)
+    all_heat_moments(2)
+    rows = gather_mx(2)
+    back2_s[:, 0, 0:128] = rows[0:n_dev]
+    back2_s[:, 0, 128:256] = rows[n_dev : 2 * n_dev]
+    landed(z1)
     inner_moments(2)
-    for copy in x1:
-        copy.wait_recv()
+    landed(x1)
     outer_moments(2)
-    fill_back(2, back2_s)
+    gather_speed(2)
+    make_drag(2)
+    back2_s[:, 0, 256:384] = drags[...]
     send_rows(5, back2_s, back2_r)
-    gather_speed(2)
-    rows_here(4, out2_r)
-    make_drag(2)
-    drag_s[:, 0, :] = drags[...]
-    send_rows(6, drag_s, drag_r)
-    make_spread(2)
     x2 = outer_flow(2)
+    h2 = heat(2)
     z2 = inner_flow(2)
     rows_here(5, back2_r)
-    grow(2, lambda s: back2_r[:, s, :])
+    grow(2, lambda s: back2_r[:, 0, s * 128 : (s + 1) * 128])
     solid_out[...] = solid[...]
-    rows_here(6, drag_r)
-    means = drag_r[:, 0, :].T
+    means = back2_r[:, 0, 256:384].T
     total = jnp.zeros((8, grains), F32)
     for t in range(3):
         for s in range(2):
@@ -507,11 +540,10 @@
             total = total + product(high, d) + product(low, d)
     drag_out[...] = total[0:3, :] * DRAG_SCALE
 
-    for copy in z2 + x2:
-        copy.wait_recv()
-    for copy in z0 + x0 + z1 + x1 + z2 + x2:
+    landed(h2 + z2 + x2)
+    for copy in h0 + x0 + z0 + h1 + x1 + z1 + h2 + x2 + z2:
         copy.wait_send()
-    sources = (out0_s, back0_s, out1_s, back1_s, out2_s, back2_s, drag_s)
+    sources = (out0_s, back0_s, out1_s, back1_s, out2_s, back2_s)
     for which, source in enumerate(sources):
         rows_sent(which, source)
 
@@ -541,7 +573,6 @@
     state = pltpu.VMEM((26, width_x + 2, width_z + 16, width_y), F32)
     wide = pltpu.VMEM((n_dev, 1, 384), F32)
     plain = pltpu.VMEM((n_dev, 2, 128), F32)
-    thin = pltpu.VMEM((n_dev, 1, 128), F32)
     plane = (width_x, width_z, width_y)
     hbm = pl.BlockSpec(memory_space=pltpu.HBM)
     operands = (
@@ -570,27 +601,31 @@
             pltpu.VMEM((3, grains), jnp.int32),
             pltpu.VMEM(plane, F32),
             pltpu.VMEM((3,) + plane, F32),
-            pltpu.VMEM(plane, F32),
+            pltpu.VMEM((2,) + plane, F32),
             pltpu.VMEM((2 * width_x, width_z, 128), BF16),
             pltpu.VMEM((2 * width_x, width_z, 384), BF16),
-            pltpu.VMEM((width_x, width_z, 640), F32),
+            pltpu.VMEM((width_x, width_z, 512), F32),
+            pltpu.VMEM(plane, F32),
             pltpu.VMEM((128, grains), F32),
             pltpu.VMEM((3, 2 * n_dev, 2 * cells), BF16),
             pltpu.VMEM((3, cells, 4 * n_dev), BF16),
             pltpu.VMEM((3, 2 * n_dev, 2 * grains), BF16),
             pltpu.VMEM((3, grains, 4 * n_dev), BF16),
             pltpu.VMEM((3, grains, 128), F32),
-            pltpu.VMEM((4 * n_dev, 640), BF16),
+            pltpu.VMEM((3, 2, 3, n_dev, 128), F32),
+            pltpu.VMEM((3, 2, n_dev, 128), F32),
+            pltpu.VMEM((4 * n_dev, 512), BF16),
+            pltpu.VMEM((4 * n_dev, 128), BF16),
             pltpu.VMEM((grains, 128), F32),
             pltpu.VMEM((n_dev, 128), F32),
             pltpu.VMEM((2 * n_dev, 384), F32),
             wide, wide, plain, plain, plain, plain,
-            plain, plain, plain, plain, plain, plain, thin, thin,
+            plain, plain, plain, plain, wide, wide,
             pltpu.SemaphoreType.DMA((31,)),
-            pltpu.SemaphoreType.DMA((48,)),
-            pltpu.SemaphoreType.DMA((48,)),
-            pltpu.SemaphoreType.DMA((7,)),
-            pltpu.SemaphoreType.DMA((7,)),
+            pltpu.SemaphoreType.DMA((60,)),
+            pltpu.SemaphoreType.DMA((60,)),
+            pltpu.SemaphoreType.DMA((6,)),
+            pltpu.SemaphoreType.DMA((6,)),
         ],
         compiler_params=pltpu.CompilerParams(
             collective_id=0, has_side_effects=True, vmem_limit_bytes=50 * 1024 * 1024

time: 56.6 us -> 52.8 us (0.933); the launches traced: 55.7 us -> 52.7 us
  Pallas kernels: 54.9 us -> 51.9 us
    pallas_call x1, Pallas kernels: 52.9 us -> 49.9 us  [on_device(): pl.pallas_call(functools.partial(kernel, sizes), out_shape=(state, pltpu....]
where the time goes in v2:
time: 52.8 us; the launch traced here: 52.7 us
  Pallas kernels  51.9 us (98%)
  between operations  0.8 us (2%)
    pallas_call x1, Pallas kernels, on_device(): pl.pallas_call(functools.partial(kernel, sizes), out_shape=(state, pltpu....  49.9 us
    pallas_call x1, Pallas kernels, on_device(): pl.pallas_call(deliver, out_shape=(jax.ShapeDtypeStruct(populations.shape...  2 us

profile of v2, /device:TPU:1, one launch (start us, length us, event | category | flops | bytes accessed | tf_op | source)
XLA Modules:
  0.0 52.7 jit_solution(7356386768023854188)
XLA Ops:
  0.6 49.9 %shard_map.102 = (f32[26,10,48,128]{3,2,1,0:T(8,128)S(1)}, f32[128,128]{1,0:T(8,128)S(1)}, f32[3,128]{1,0:T(4,128)S(1)}) custom-call(f32[19,8,32,128]{3,2,1,0:T(8,128)} %pop.1, f32[7,8,32,128]{3,2,1,0:T(8,128)} %th.1, f32[128,128]{1,0:T(8,128)} %solid_in.1, s32[3,1,128]{2,1,0:T(1,128)} %bitcast.1, s32[3,128]{1,0:T(4,128)} %ccol_in.1, s32[3,3,128]{2,1,0:T(4,128)} %gvel_in.1, ...), custom_call_target="tpu_custom_call" | custom-call | tf_op jit(solution)/shard_map/pallas_call | solution.py:587
  50.6 2.0 %shard_map.103 = (f32[19,8,32,128]{3,2,1,0:T(8,128)}, f32[7,8,32,128]{3,2,1,0:T(8,128)}, f32[128,128]{1,0:T(8,128)}, f32[3,128]{1,0:T(4,128)}) custom-call(f32[26,10,48,128]{3,2,1,0:T(8,128)S(1)} %get-tuple-element.7.state, f32[128,128]{1,0:T(8,128)S(1)} %get-tuple-element.8.solid, f32[3,128]{1,0:T(4,128)S(1)} %get-tuple-element.9.drag), custom_call_target="tpu_custom_call" | custom-call | tf_op jit(solution)/shard_map/pallas_call | solution.py:634

commit v3 on v2

--- a/solution.py
+++ b/solution.py
@@ -470,14 +470,14 @@
     x0 = outer_flow(0)
     make_pick(1)
     inner_cover(0)
+    rows_here(1, back0_r)
+    grow(0, lambda s: back0_r[:, s, :])
+    pack_rows(1, out1_s)
+    send_rows(2, out1_s, out1_r)
     landed(h0)
     all_heat_moments(1)
     fill_back(1, back1_s)
     send_rows(3, back1_s, back1_r)
-    rows_here(1, back0_r)
-    grow(0, lambda s: back0_r[:, s, :])
-    pack_rows(1, out1_s)
-    send_rows(2, out1_s, out1_r)
     z0 = inner_flow(0)
     gather_speed(0)
     make_drag(0)
@@ -492,24 +492,19 @@
     outer_moments(1)
     gather_speed(1)
 
+    rows_here(2, out1_r)
+    make_spread(1)
+    outer_cover(1)
+    x1 = outer_flow(1)
     rows_here(3, back1_r)
     grow(1, lambda s: back1_r[:, s, :])
     pack_rows(2, out2_s)
     send_rows(4, out2_s, out2_r)
-    rows_here(2, out1_r)
-    make_spread(1)
-    outer_cover(1)
-    x1 = outer_flow(1)
     heat_cover(1)
     h1 = heat(1)
     inner_cover(1)
     z1 = inner_flow(1)
     make_drag(1)
-    rows_here(4, out2_r)
-    make_spread(2)
-    outer_cover(2)
-    inner_cover(2)
-    heat_cover(2)
 
     landed(h1)
     all_heat_moments(2)
@@ -521,11 +516,16 @@
     landed(x1)
     outer_moments(2)
     gather_speed(2)
+    rows_here(4, out2_r)
     make_drag(2)
     back2_s[:, 0, 256:384] = drags[...]
     send_rows(5, back2_s, back2_r)
+    make_spread(2)
+    outer_cover(2)
     x2 = outer_flow(2)
+    heat_cover(2)
     h2 = heat(2)
+    inner_cover(2)
     z2 = inner_flow(2)
     rows_here(5, back2_r)
     grow(2, lambda s: back2_r[:, 0, s * 128 : (s + 1) * 128])

time: 52.8 us -> 52.2 us (0.989)
  Pallas kernels: 51.9 us -> 51.3 us
    pallas_call x1, Pallas kernels: 49.9 us -> 49.3 us  [on_device(): pl.pallas_call(functools.partial(kernel, sizes), out_shape=(state, pltpu....]
where the time goes in v3:
time: 52.2 us; the launch traced here: 52.1 us
  Pallas kernels  51.3 us (98%)
  between operations  0.8 us (2%)
    pallas_call x1, Pallas kernels, on_device(): pl.pallas_call(functools.partial(kernel, sizes), out_shape=(state, pltpu....  49.3 us
    pallas_call x1, Pallas kernels, on_device(): pl.pallas_call(deliver, out_shape=(jax.ShapeDtypeStruct(populations.shape...  2 us

profile of v3, /device:TPU:1, one launch (start us, length us, event | category | flops | bytes accessed | tf_op | source)
XLA Modules:
  0.0 52.1 jit_solution(3569942941412751568)
XLA Ops:
  0.6 49.3 %shard_map.102 = (f32[26,10,48,128]{3,2,1,0:T(8,128)S(1)}, f32[128,128]{1,0:T(8,128)S(1)}, f32[3,128]{1,0:T(4,128)S(1)}) custom-call(f32[19,8,32,128]{3,2,1,0:T(8,128)} %pop.1, f32[7,8,32,128]{3,2,1,0:T(8,128)} %th.1, f32[128,128]{1,0:T(8,128)} %solid_in.1, s32[3,1,128]{2,1,0:T(1,128)} %bitcast.1, s32[3,128]{1,0:T(4,128)} %ccol_in.1, s32[3,3,128]{2,1,0:T(4,128)} %gvel_in.1, ...), custom_call_target="tpu_custom_call" | custom-call | tf_op jit(solution)/shard_map/pallas_call | solution.py:587
  49.9 2.0 %shard_map.103 = (f32[19,8,32,128]{3,2,1,0:T(8,128)}, f32[7,8,32,128]{3,2,1,0:T(8,128)}, f32[128,128]{1,0:T(8,128)}, f32[3,128]{1,0:T(4,128)}) custom-call(f32[26,10,48,128]{3,2,1,0:T(8,128)S(1)} %get-tuple-element.7.state, f32[128,128]{1,0:T(8,128)S(1)} %get-tuple-element.8.solid, f32[3,128]{1,0:T(4,128)S(1)} %get-tuple-element.9.drag), custom_call_target="tpu_custom_call" | custom-call | tf_op jit(solution)/shard_map/pallas_call | solution.py:634

commit v4 on v3

--- a/solution.py
+++ b/solution.py
@@ -405,7 +405,10 @@
 
     def halo(t, first, faces):
         copies = []
-        for j, (k, x_from, z_from, x_to, z_to, to) in enumerate(faces):
+        for j, face in enumerate(faces):
+            if face is None:
+                continue
+            k, x_from, z_from, x_to, z_to, to = face
             copies.append(
                 pltpu.make_async_remote_copy(
                     src_ref=states[t + 1].at[k, x_from, z_from, :],
@@ -420,8 +423,11 @@
         return copies
 
     def outer_flow(t):
-        over(2, 0, width_x - 1, lambda x: collide_flow(t, x))
-        return halo(t, 0, faces_x)
+        copies = []
+        for x, side in ((width_x - 1, right), (0, left)):
+            over(1, x, 1, lambda x: collide_flow(t, x))
+            copies += halo(t, 0, [face if face[5][0] is side else None for face in faces_x])
+        return copies
 
     def inner_flow(t):
         over(width_x - 2, 1, 1, lambda x: collide_flow(t, x))

time: 52.2 us -> 52 us (level)
  no operation moved by 1% of the time
where the time goes in v4:
time: 52 us; the launch traced here: 51.9 us
  Pallas kernels  51.1 us (98%)
  between operations  0.8 us (2%)
    pallas_call x1, Pallas kernels, on_device(): pl.pallas_call(functools.partial(kernel, sizes), out_shape=(state, pltpu....  49.1 us
    pallas_call x1, Pallas kernels, on_device(): pl.pallas_call(deliver, out_shape=(jax.ShapeDtypeStruct(populations.shape...  2 us

profile of v4, /device:TPU:1, one launch (start us, length us, event | category | flops | bytes accessed | tf_op | source)
XLA Modules:
  0.0 51.9 jit_solution(15387611750747480667)
XLA Ops:
  0.6 49.1 %shard_map.102 = (f32[26,10,48,128]{3,2,1,0:T(8,128)S(1)}, f32[128,128]{1,0:T(8,128)S(1)}, f32[3,128]{1,0:T(4,128)S(1)}) custom-call(f32[19,8,32,128]{3,2,1,0:T(8,128)} %pop.1, f32[7,8,32,128]{3,2,1,0:T(8,128)} %th.1, f32[128,128]{1,0:T(8,128)} %solid_in.1, s32[3,1,128]{2,1,0:T(1,128)} %bitcast.1, s32[3,128]{1,0:T(4,128)} %ccol_in.1, s32[3,3,128]{2,1,0:T(4,128)} %gvel_in.1, ...), custom_call_target="tpu_custom_call" | custom-call | tf_op jit(solution)/shard_map/pallas_call | solution.py:593
  49.7 2.0 %shard_map.103 = (f32[19,8,32,128]{3,2,1,0:T(8,128)}, f32[7,8,32,128]{3,2,1,0:T(8,128)}, f32[128,128]{1,0:T(8,128)}, f32[3,128]{1,0:T(4,128)}) custom-call(f32[26,10,48,128]{3,2,1,0:T(8,128)S(1)} %get-tuple-element.7.state, f32[128,128]{1,0:T(8,128)S(1)} %get-tuple-element.8.solid, f32[3,128]{1,0:T(4,128)S(1)} %get-tuple-element.9.drag), custom_call_target="tpu_custom_call" | custom-call | tf_op jit(solution)/shard_map/pallas_call | solution.py:640
